TPU v7x, 512 devices: a whole 4x4x16 slice. The times are simulated.
512 devices in a mesh: blk: 32 (over z, core), row: 16 (over x, y).
Axes of the slice: x: 4, y: 4, z: 16, core: 2. Of those that a mesh axis runs over, the one named last changes fastest.
Arguments:
- load_cases: float32 [32, 1536, 512], P('blk', 'row'), may hold values from -6 to 6
- lower_factor: bfloat16 [32, 5, 1536, 1536], P('blk', None, 'row'), may hold values from -0.0390625 to 0.0390625
- upper_factor: bfloat16 [32, 5, 1536, 1536], P('blk', None, 'row'), may hold values from -0.0390625 to 0.0390625
- inverse: bfloat16 [32, 1536, 1536], P('blk', 'row'), may hold values from -2 to 2, as said below
Outputs:
- response: float32 [32, 1536, 512], P('blk', 'row')
Inputs may be any that keep to these rules, and one draw needn't show every extreme that they name: `inverse`: each block has its diagonal entries between 0.4 and 2 and small off-diagonal entries.
All inputs are finite; a program needn't handle non-finite values.
Results may differ from a plain program's by a relative error of at most 0.0035.
Values may be sent and summed in bfloat16 or wider, within the bound.
A program may use at most 64 MiB of HBM per device.

v0:
```python
import jax
import jax.numpy as jnp
from jax import lax
from jax.sharding import PartitionSpec as P


def passed_along(value, axis, steps):
    count = lax.axis_size(axis)
    leading, last = (max(0, -steps), min(count, count - steps))
    return lax.ppermute(value, axis, [(source, source + steps) for source in range(leading, last)])


def product(block, vectors):
    return jnp.dot(block, vectors, preferred_element_type=jnp.float32)


def subtract_columns(below_block, above_block, running, pieces):
    return running - product(below_block, pieces[0]) - product(above_block, pieces[1])


def add_columns(inverse_block, shard_piece):
    return product(inverse_block, shard_piece)


def per_device(load_cases, lower_factor, upper_factor, inverse):
    levels = lax.axis_size("blk").bit_length() - 1
    current = load_cases[0]
    below_all = lower_factor[0]
    above_all = upper_factor[0]
    for level_index in range(levels):
        distance = 2**level_index
        rounded = current.astype(jnp.bfloat16)
        neighbours = [passed_along(rounded, "blk", offset) for offset in (distance, -distance)]
        current = subtract_columns(
            below_all[level_index],
            above_all[level_index],
            current,
            (
                lax.all_gather(neighbours[0], "row", axis=0, tiled=True),
                lax.all_gather(neighbours[1], "row", axis=0, tiled=True),
            ),
        )
    rounded = current.astype(jnp.bfloat16)
    answer = add_columns(inverse[0], lax.all_gather(rounded, "row", axis=0, tiled=True))
    return answer[None]


def solution(mesh):
    return jax.shard_map(
        per_device,
        mesh=mesh,
        in_specs=(
            P("blk", "row", None),
            P("blk", None, "row", None),
            P("blk", None, "row", None),
            P("blk", "row", None),
        ),
        out_specs=P("blk", "row", None),
        check_vma=False,
    )
```

profile of v0, /device:TPU:1, one launch (start us, length us, event | category | flops | bytes accessed | tf_op | source)
XLA Modules:
  0.0 750.8 jit_solution(7994648972397798415)
XLA Ops:
  7.6 8.8 %collective-permute-start.1 = (bf16[96,512]{1,0:T(8,128)(2,1)S(1)}, bf16[96,512]{1,0:T(8,128)(2,1)S(1)}, u32[]{:S(2)}, u32[]{:S(2)}) collective-permute-start(bf16[96,512]{1,0:T(8,128)(2,1)S(1)} %bitcast_convert_fusion), channel_id=1, source_target_pairs={{16,0},{32,16},{48,32},{64,48},{80,64},{96,80},{112,96},{128,112},... | collective-permute-start | bytes 294920 | tf_op jit(solution)/shard_map/ppermute | solution.py:10
  22.3 55.1 %all-gather.14.cloned.1.call-done = bf16[1536,512]{1,0:T(8,128)(2,1)} async-done(((bf16[96,512]{1,0:T(8,128)(2,1)}), bf16[1536,512]{1,0:T(8,128)(2,1)}) %all-gather.14.cloned.1.call-update) | async-done | bytes 1572880 | tf_op jit(solution)/shard_map/all_gather | solution.py:40
  77.5 2.6 fusion.19
  80.1 59.2 %all-gather.12.cloned.1.call-done = bf16[1536,512]{1,0:T(8,128)(2,1)} async-done(((bf16[96,512]{1,0:T(8,128)(2,1)}), bf16[1536,512]{1,0:T(8,128)(2,1)}) %all-gather.12.cloned.1.call-update) | async-done | bytes 1572880 | tf_op jit(solution)/shard_map/all_gather | solution.py:39
  139.3 2.5 fusion.32
  143.1 4.1 collective-permute-done.3
  147.8 3.2 collective-permute-start.2
  153.4 54.4 %all-gather.18.cloned.1.call-done = bf16[1536,512]{1,0:T(8,128)(2,1)} async-done(((bf16[96,512]{1,0:T(8,128)(2,1)}), bf16[1536,512]{1,0:T(8,128)(2,1)}) %all-gather.18.cloned.1.call-update) | async-done | bytes 1572880 | tf_op jit(solution)/shard_map/all_gather | solution.py:40
  210.3 59.2 %all-gather.16.cloned.1.call-done = bf16[1536,512]{1,0:T(8,128)(2,1)} async-done(((bf16[96,512]{1,0:T(8,128)(2,1)}), bf16[1536,512]{1,0:T(8,128)(2,1)}) %all-gather.16.cloned.1.call-update) | async-done | bytes 1572880 | tf_op jit(solution)/shard_map/all_gather | solution.py:39
  272.7 5.1 collective-permute-done.5
  277.8 6.1 collective-permute-start.4
  285.1 53.9 %all-gather.22.cloned.1.call-done = bf16[1536,512]{1,0:T(8,128)(2,1)} async-done(((bf16[96,512]{1,0:T(8,128)(2,1)}), bf16[1536,512]{1,0:T(8,128)(2,1)}) %all-gather.22.cloned.1.call-update) | async-done | bytes 1572880 | tf_op jit(solution)/shard_map/all_gather | solution.py:40
  341.4 59.2 %all-gather.20.cloned.1.call-done = bf16[1536,512]{1,0:T(8,128)(2,1)} async-done(((bf16[96,512]{1,0:T(8,128)(2,1)}), bf16[1536,512]{1,0:T(8,128)(2,1)}) %all-gather.20.cloned.1.call-update) | async-done | bytes 1572880 | tf_op jit(solution)/shard_map/all_gather | solution.py:39
  400.6 2.5 fusion.34
  404.5 8.2 %collective-permute-done.7 = bf16[96,512]{1,0:T(8,128)(2,1)} collective-permute-done((bf16[96,512]{1,0:T(8,128)(2,1)S(1)}, bf16[96,512]{1,0:T(8,128)(2,1)}, u32[]{:S(2)}, u32[]{:S(2)}) %collective-permute-start.7) | collective-permute-done | bytes 98336 | tf_op jit(solution)/shard_map/ppermute | solution.py:10
  412.8 12.4 %collective-permute-start.6 = (bf16[96,512]{1,0:T(8,128)(2,1)S(1)}, bf16[96,512]{1,0:T(8,128)(2,1)}, u32[]{:S(2)}, u32[]{:S(2)}) collective-permute-start(bf16[96,512]{1,0:T(8,128)(2,1)S(1)} %get-tuple-element.9), channel_id=1, source_target_pairs={{0,128},{16,144},{32,160},{48,176},{64,192},{80,208},{96,224},{112... | collective-permute-start | bytes 294920 | tf_op jit(solution)/shard_map/ppermute | solution.py:10
  426.3 51.7 %all-gather.26.cloned.1.call-done = bf16[1536,512]{1,0:T(8,128)(2,1)} async-done(((bf16[96,512]{1,0:T(8,128)(2,1)}), bf16[1536,512]{1,0:T(8,128)(2,1)}) %all-gather.26.cloned.1.call-update) | async-done | bytes 1572880 | tf_op jit(solution)/shard_map/all_gather | solution.py:40
  480.4 59.3 %all-gather.24.cloned.1.call-done = bf16[1536,512]{1,0:T(8,128)(2,1)} async-done(((bf16[96,512]{1,0:T(8,128)(2,1)}), bf16[1536,512]{1,0:T(8,128)(2,1)}) %all-gather.24.cloned.1.call-update) | async-done | bytes 1572880 | tf_op jit(solution)/shard_map/all_gather | solution.py:39
  539.8 2.5 fusion.35
  543.6 13.1 %collective-permute-done.9 = bf16[96,512]{1,0:T(8,128)(2,1)} collective-permute-done((bf16[96,512]{1,0:T(8,128)(2,1)S(1)}, bf16[96,512]{1,0:T(8,128)(2,1)}, u32[]{:S(2)}, u32[]{:S(2)}) %collective-permute-start.9) | collective-permute-done | bytes 98336 | tf_op jit(solution)/shard_map/ppermute | solution.py:10
  558.8 6.3 collective-permute-done.8
  565.2 53.2 %all-gather.30.cloned.1.call-done = bf16[1536,512]{1,0:T(8,128)(2,1)} async-done(((bf16[96,512]{1,0:T(8,128)(2,1)}), bf16[1536,512]{1,0:T(8,128)(2,1)}) %all-gather.30.cloned.1.call-update) | async-done | bytes 1572880 | tf_op jit(solution)/shard_map/all_gather | solution.py:40
  620.8 59.2 %all-gather.28.cloned.1.call-done = bf16[1536,512]{1,0:T(8,128)(2,1)} async-done(((bf16[96,512]{1,0:T(8,128)(2,1)}), bf16[1536,512]{1,0:T(8,128)(2,1)}) %all-gather.28.cloned.1.call-update) | async-done | bytes 1572880 | tf_op jit(solution)/shard_map/all_gather | solution.py:39
  682.5 59.3 %all-gather.32.cloned.1.call-done = bf16[1536,512]{1,0:T(8,128)(2,1)} async-done(((bf16[96,512]{1,0:T(8,128)(2,1)}), bf16[1536,512]{1,0:T(8,128)(2,1)}) %all-gather.32.cloned.1.call-update) | async-done | bytes 1572880 | tf_op jit(solution)/shard_map/all_gather | solution.py:44
  (61 shorter events, 36.4 us)
Async XLA Ops:
  6.5 735.3 %copy-start = (bf16[1,96,1536]{2,1,0:T(8,128)(2,1)S(1)}, bf16[1,96,1536]{2,1,0:T(8,128)(2,1)}, u32[]{:S(2)}) copy-start(bf16[1,96,1536]{2,1,0:T(8,128)(2,1)} %param.7) | copy-start | bytes 884740
  6.5 70.9 %all-gather.14.cloned.1.call-start = ((), (), s32[]{:S(2)}) async-start(), calls=%async_computation.1 | async-start | bytes 1671168 | tf_op jit(solution)/shard_map/all_gather | solution.py:40
  7.6 9.7 %collective-permute-start.1 = (bf16[96,512]{1,0:T(8,128)(2,1)S(1)}, bf16[96,512]{1,0:T(8,128)(2,1)S(1)}, u32[]{:S(2)}, u32[]{:S(2)}) collective-permute-start(bf16[96,512]{1,0:T(8,128)(2,1)S(1)} %bitcast_convert_fusion), channel_id=1, source_target_pairs={{16,0},{32,16},{48,32},{64,48},{80,64},{96,80},{112,96},{128,112},... | collective-permute-start | bytes 294920 | tf_op jit(solution)/shard_map/ppermute | solution.py:10
  18.0 121.3 %all-gather.12.cloned.1.call-start = ((), (), s32[]{:S(2)}) async-start(), calls=%async_computation | async-start | bytes 1671168 | tf_op jit(solution)/shard_map/all_gather | solution.py:39
  18.1 3.5 collective-permute-start
  22.3 185.5 %all-gather.18.cloned.1.call-start = ((), (), s32[]{:S(2)}) async-start(), calls=%async_computation.3 | async-start | bytes 1671168 | tf_op jit(solution)/shard_map/all_gather | solution.py:40
  141.8 5.3 collective-permute-start.3
  147.8 121.7 %all-gather.16.cloned.1.call-start = ((), (), s32[]{:S(2)}) async-start(), calls=%async_computation.2 | async-start | bytes 1671168 | tf_op jit(solution)/shard_map/all_gather | solution.py:39
  147.8 4.8 collective-permute-start.2
  153.3 185.6 %all-gather.22.cloned.1.call-start = ((), (), s32[]{:S(2)}) async-start(), calls=%async_computation.5 | async-start | bytes 1671168 | tf_op jit(solution)/shard_map/all_gather | solution.py:40
  271.4 6.4 collective-permute-start.5
  277.8 122.8 %all-gather.20.cloned.1.call-start = ((), (), s32[]{:S(2)}) async-start(), calls=%async_computation.4 | async-start | bytes 1671168 | tf_op jit(solution)/shard_map/all_gather | solution.py:39
  277.8 7.1 collective-permute-start.4
  285.0 192.9 %all-gather.26.cloned.1.call-start = ((), (), s32[]{:S(2)}) async-start(), calls=%async_computation.7 | async-start | bytes 1671168 | tf_op jit(solution)/shard_map/all_gather | solution.py:40
  403.1 136.7 %copy-start.3 = (f32[96,512]{1,0:T(8,128)S(1)}, f32[96,512]{1,0:T(8,128)}, u32[]{:S(2)}) copy-start(f32[96,512]{1,0:T(8,128)} %get-tuple-element.10) | copy-start | bytes 589828
  403.1 9.6 %collective-permute-start.7 = (bf16[96,512]{1,0:T(8,128)(2,1)S(1)}, bf16[96,512]{1,0:T(8,128)(2,1)}, u32[]{:S(2)}, u32[]{:S(2)}) collective-permute-start(bf16[96,512]{1,0:T(8,128)(2,1)S(1)} %get-tuple-element.9), channel_id=1, source_target_pairs={{128,0},{144,16},{160,32},{176,48},{192,64},{208,80},{224,96},{240... | collective-permute-start | bytes 294920 | tf_op jit(solution)/shard_map/ppermute | solution.py:10
  412.7 127.0 %all-gather.24.cloned.1.call-start = ((), (), s32[]{:S(2)}) async-start(), calls=%async_computation.6 | async-start | bytes 1671168 | tf_op jit(solution)/shard_map/all_gather | solution.py:39
  412.8 13.4 %collective-permute-start.6 = (bf16[96,512]{1,0:T(8,128)(2,1)S(1)}, bf16[96,512]{1,0:T(8,128)(2,1)}, u32[]{:S(2)}, u32[]{:S(2)}) collective-permute-start(bf16[96,512]{1,0:T(8,128)(2,1)S(1)} %get-tuple-element.9), channel_id=1, source_target_pairs={{0,128},{16,144},{32,160},{48,176},{64,192},{80,208},{96,224},{112... | collective-permute-start | bytes 294920 | tf_op jit(solution)/shard_map/ppermute | solution.py:10
  426.2 192.1 %all-gather.30.cloned.1.call-start = ((), (), s32[]{:S(2)}) async-start(), calls=%async_computation.9 | async-start | bytes 1671168 | tf_op jit(solution)/shard_map/all_gather | solution.py:40
  542.2 137.8 %copy-start.4 = (f32[96,512]{1,0:T(8,128)S(1)}, f32[96,512]{1,0:T(8,128)}, u32[]{:S(2)}) copy-start(f32[96,512]{1,0:T(8,128)} %get-tuple-element.12) | copy-start | bytes 589828
  542.2 14.5 %collective-permute-start.9 = (bf16[96,512]{1,0:T(8,128)(2,1)S(1)}, bf16[96,512]{1,0:T(8,128)(2,1)}, u32[]{:S(2)}, u32[]{:S(2)}) collective-permute-start(bf16[96,512]{1,0:T(8,128)(2,1)S(1)} %get-tuple-element.11), channel_id=1, source_target_pairs={{256,0},{272,16},{288,32},{304,48},{320,64},{336,80},{352,96},{368... | collective-permute-start | bytes 294920 | tf_op jit(solution)/shard_map/ppermute | solution.py:10
  556.8 123.2 %all-gather.28.cloned.1.call-start = ((), (), s32[]{:S(2)}) async-start(), calls=%async_computation.8 | async-start | bytes 1671168 | tf_op jit(solution)/shard_map/all_gather | solution.py:39
  556.9 8.2 %collective-permute-start.8 = (bf16[96,512]{1,0:T(8,128)(2,1)S(1)}, bf16[96,512]{1,0:T(8,128)(2,1)}, u32[]{:S(2)}, u32[]{:S(2)}) collective-permute-start(bf16[96,512]{1,0:T(8,128)(2,1)S(1)} %get-tuple-element.11), channel_id=1, source_target_pairs={{0,256},{16,272},{32,288},{48,304},{64,320},{80,336},{96,352},{112... | collective-permute-start | bytes 294920 | tf_op jit(solution)/shard_map/ppermute | solution.py:10
  565.1 176.7 %all-gather.32.cloned.1.call-start = ((), (), s32[]{:S(2)}) async-start(), calls=%async_computation.10 | async-start | bytes 1671168 | tf_op jit(solution)/shard_map/all_gather | solution.py:44
  (7 other events, 395.8 us)
Sparse Core Ops, SparseCore 0:
  18.1 59.2 all-gather.13
  80.5 58.7 all-gather.11
  147.9 59.8 all-gather.17
  210.7 58.7 all-gather.15
  277.9 60.9 all-gather.21
  341.9 58.7 all-gather.19
  412.8 65.0 all-gather.25
  481.0 58.7 all-gather.23
  556.9 61.3 all-gather.29
  621.3 58.7 all-gather.27
  683.1 58.7 all-gather.31
where the time goes:
time: 751 us
  waiting for transfers between devices  667 us (89%)
  starting transfers between devices  40.2 us (5%)
  matrix products  26.7 us (4%)
  between operations  13.3 us (2%)
    all_gather x5, waiting for transfers between devices, per_device(): lax.all_gather(neighbours[0], 'row', axis=0, tiled=True)  296 us
    all_gather x5, waiting for transfers between devices, per_device(): lax.all_gather(neighbours[1], 'row', axis=0, tiled=True)  268 us
    all_gather x1, waiting for transfers between devices, per_device(): lax.all_gather(rounded, 'row', axis=0, tiled=True)  59.3 us
    ppermute x10, waiting for transfers between devices, passed_along(): lax.ppermute(value, axis, [(source, source + steps) for source in range(l...  42.9 us
    ppermute x10, starting transfers between devices, passed_along(): lax.ppermute(value, axis, [(source, source + steps) for source in range(l...  39.8 us
    dot_general x11, matrix products, product(): return jnp.dot(block, vectors, preferred_element_type=jnp.float32)  26.7 us
  transfers between devices with their start and end apart: 21, of which 21 were waited for; matrix products, arithmetic and copies ran while one was open for 2% of the time, Pallas kernels for 0%

commit v1 on v0

v1 whole, which is shorter than its diff:
```python
import jax
import jax.numpy as jnp
from jax import lax
from jax.experimental import pallas as pl
from jax.experimental.pallas import tpu as pltpu
from jax.sharding import PartitionSpec as P

MESH = pl.DeviceIdType.MESH
LEVELS = 5
FRAMES = 32
SIDE = 4
ROWS = 96
WIDTH = 128
CHUNKS = 4
FUSED = (0, 1, 2)
LAST = LEVELS


def units(level):
    if level < LEVELS - 1:
        return [(2 * level, 2**level), (2 * level + 1, -(2**level))]
    if level == LEVELS - 1:
        return [(2 * level, FRAMES // 2)]
    return [(2 * LEVELS - 1, 0)]


def kernel(load, lower, upper, inverse, out, fac, inv, cur, own, gat, fac_sem, z_sem, a_sem, b_sem, far_sem, send_sem, last_sem):
    frame = lax.axis_index("blk")
    row = lax.axis_index("row")
    x, y = row // SIDE, row % SIDE

    def device(shift, dx, dy):
        return ((frame + shift + FRAMES) % FRAMES, ((x + dx) % SIDE) * SIDE + (y + dy) % SIDE)

    loads = [
        pltpu.make_async_copy(lower.at[0], fac.at[0], fac_sem.at[0]),
        pltpu.make_async_copy(upper.at[0], fac.at[1], fac_sem.at[1]),
        pltpu.make_async_copy(inverse.at[0], inv, fac_sem.at[2]),
    ]
    for copy in loads:
        copy.start()

    partners = {(0, d, 0) for d in range(1, SIDE)} | {(0, 0, d) for d in range(1, SIDE)}
    for level in range(LEVELS):
        for _, shift in units(level):
            partners.add((shift, 0, 0))
            if level in FUSED:
                for d in range(1, SIDE):
                    partners |= {(shift, d, 0), (shift, 0, d)}
    barrier = pltpu.get_barrier_semaphore()
    for partner in sorted(partners):
        pl.semaphore_signal(barrier, inc=1, device_id=device(*partner), device_id_type=MESH)

    def along(level, chunk, index):
        return index if level < LEVELS - 1 else chunk % 2

    def step(turn, d):
        return (d, 0) if turn == 0 else (0, d)

    def line(u, c, turn, at, first=0, count=SIDE):
        if turn == 0:
            return gat.at[u, c, pl.ds(first, count), at]
        return gat.at[u, c, at, pl.ds(first, count)]

    def send(src, dst, sem, recv, to):
        pltpu.make_async_remote_copy(src_ref=src, dst_ref=dst, send_sem=sem, recv_sem=recv, device_id=to, device_id_type=MESH).start()

    def wait(ref, sem):
        pltpu.make_async_copy(ref, ref, sem).wait()

    def begin(level, c):
        value = cur[c].astype(jnp.bfloat16)
        if level == LAST:
            u, _ = units(level)[0]
            turn = along(level, c, 0)
            gat[u, c, x, y] = value
            for d in (2, 1, 3):
                send(gat.at[u, c, x, y], gat.at[u, c, x, y], last_sem.at[c], a_sem.at[u, c], device(0, *step(turn, d)))
            return
        own[level, c] = value
        for i, (u, shift) in enumerate(units(level)):
            turn = along(level, c, i)
            if level in FUSED:
                for d in (2, 1, 3, 0):
                    send(own.at[level, c], gat.at[u, c, x, y], send_sem.at[level, c], a_sem.at[u, c], device(shift, *step(turn, d)))
            else:
                send(own.at[level, c], gat.at[u, c, x, y], send_sem.at[level, c], z_sem.at[u, c], device(shift, 0, 0))

    def spread(level, c):
        if level in FUSED or level == LAST:
            return
        for i, (u, _) in enumerate(units(level)):
            turn = along(level, c, i)
            wait(gat.at[u, c, x, y], z_sem.at[u, c])
            for d in (2, 1, 3):
                send(gat.at[u, c, x, y], gat.at[u, c, x, y], send_sem.at[level, c], a_sem.at[u, c], device(0, *step(turn, d)))

    def cross(level, c):
        for i, (u, _) in enumerate(units(level)):
            turn = along(level, c, i)
            at = y if turn == 0 else x
            wait(line(u, c, turn, at, 0, SIDE if level in FUSED else SIDE - 1), a_sem.at[u, c])
            for d in (1, SIDE - 1):
                block = line(u, c, turn, at)
                send(block, block, send_sem.at[level, c], b_sem.at[u, c], device(0, *step(1 - turn, d)))

    def relay(level, c):
        for i, (u, _) in enumerate(units(level)):
            turn = along(level, c, i)
            at = y if turn == 0 else x
            wait(line(u, c, turn, pl.ds(0, 2)), b_sem.at[u, c])
            for half, d in ((0, 1), (1, SIDE - 1)):
                block = line(u, c, turn, (at + SIDE - d) % SIDE, half * 2, 2)
                send(block, block, send_sem.at[level, c], far_sem.at[u, c], device(0, *step(1 - turn, d)))

    def product(block, u, c):
        return jnp.dot(block, gat[u, c].reshape(SIDE * SIDE * ROWS, WIDTH), preferred_element_type=jnp.float32)

    def finish(level, c):
        for i, (u, _) in enumerate(units(level)):
            turn = along(level, c, i)
            wait(line(u, c, turn, 0), far_sem.at[u, c])
        if level < LEVELS - 1:
            total = cur[c]
            (u, shift), (v, _) = units(level)
            total = total - jnp.where(frame >= shift, product(fac[0, level], u, c), 0.0)
            total = total - jnp.where(frame < FRAMES - shift, product(fac[1, level], v, c), 0.0)
            cur[c] = total
        elif level == LEVELS - 1:
            u, shift = units(level)[0]
            side = 1 - frame // shift
            cur[c] = cur[c] - product(fac[side, level], u, c)
        else:
            u, _ = units(level)[0]
            out[0, :, pl.ds(c * WIDTH, WIDTH)] = product(inv[...], u, c)

    for c in range(CHUNKS):
        cur[c] = load[0, :, pl.ds(c * WIDTH, WIDTH)]
    pl.semaphore_wait(barrier, len(partners))
    for c in range(CHUNKS):
        begin(0, c)
    for copy in loads:
        copy.wait()
    for level in range(LEVELS + 1):
        for c in range(CHUNKS):
            spread(level, c)
        for c in range(CHUNKS):
            cross(level, c)
        for c in range(CHUNKS):
            relay(level, c)
        for c in range(CHUNKS):
            finish(level, c)
            if level < LAST:
                begin(level + 1, c)
    for level in range(LEVELS + 1):
        for c in range(CHUNKS):
            u = units(level)[0][0]
            if level < LEVELS - 1:
                wait(gat.at[pl.ds(u, 2), c], send_sem.at[level, c])
            elif level == LEVELS - 1:
                wait(gat.at[u, c], send_sem.at[level, c])
            else:
                wait(gat.at[u, c, 0, pl.ds(0, SIDE - 1)], last_sem.at[c])
                wait(gat.at[u, c, pl.ds(0, SIDE - 1)], send_sem.at[level, c])


def per_device(load_cases, lower_factor, upper_factor, inverse):
    count = 2 * LEVELS
    return pl.pallas_call(
        kernel,
        out_shape=jax.ShapeDtypeStruct((1, ROWS, CHUNKS * WIDTH), jnp.float32),
        in_specs=[pl.BlockSpec(memory_space=pltpu.VMEM)] + [pl.BlockSpec(memory_space=pl.ANY)] * 3,
        out_specs=pl.BlockSpec(memory_space=pltpu.VMEM),
        scratch_shapes=[
            pltpu.VMEM((2, LEVELS, ROWS, SIDE * SIDE * ROWS), jnp.bfloat16),
            pltpu.VMEM((ROWS, SIDE * SIDE * ROWS), jnp.bfloat16),
            pltpu.VMEM((CHUNKS, ROWS, WIDTH), jnp.float32),
            pltpu.VMEM((LEVELS, CHUNKS, ROWS, WIDTH), jnp.bfloat16),
            pltpu.VMEM((count, CHUNKS, SIDE, SIDE, ROWS, WIDTH), jnp.bfloat16),
            pltpu.SemaphoreType.DMA((3,)),
            pltpu.SemaphoreType.DMA((count, CHUNKS)),
            pltpu.SemaphoreType.DMA((count, CHUNKS)),
            pltpu.SemaphoreType.DMA((count, CHUNKS)),
            pltpu.SemaphoreType.DMA((count, CHUNKS)),
            pltpu.SemaphoreType.DMA((LEVELS + 1, CHUNKS)),
            pltpu.SemaphoreType.DMA((CHUNKS,)),
        ],
        compiler_params=pltpu.CompilerParams(collective_id=0, has_side_effects=True, vmem_limit_bytes=48 * 2**20),
        cost_estimate=pl.CostEstimate(flops=1_660_000_000, bytes_accessed=3_700_000, transcendentals=0),
        name="hull_solve",
    )(load_cases, lower_factor, upper_factor, inverse)


def solution(mesh):
    return jax.shard_map(
        per_device,
        mesh=mesh,
        in_specs=(
            P("blk", "row", None),
            P("blk", None, "row", None),
            P("blk", None, "row", None),
            P("blk", "row", None),
        ),
        out_specs=P("blk", "row", None),
        check_vma=False,
    )
```

time: 751 us -> 148 us (0.20)
  the two profiles are of different devices: /device:TPU:1 before, /device:TPU:2 now
where the time goes in v1:
time: 148 us
  Pallas kernels  143 us (97%)
  local copies, waits for them, and re-layouts  5.31 us (4%)
    pallas_call x1, Pallas kernels, per_device(): pl.pallas_call(kernel, out_shape=jax.ShapeDtypeStruct((1, ROWS, CHUNKS *...  143 us
    unnamed x9, local copies, waits for them, and re-layouts  5.31 us

profile of v1, /device:TPU:2, one launch (start us, length us, event | category | flops | bytes accessed | tf_op | source)
XLA Modules:
  0.0 147.9 jit_solution(17707547167294947634)
XLA Ops:
  0.0 0.0 copy-start
  0.0 1.4 copy-done
  1.4 0.0 copy-start.1
  1.4 1.4 copy-done.1
  2.7 0.0 copy-start.2
  2.8 1.0 copy-done.2
  3.7 0.0 copy-start.3
  3.7 0.9 copy-done.3
  4.6 142.6 %hull_solve.1 = f32[1,96,512]{2,1,0:T(8,128)S(1)} custom-call(f32[1,96,512]{2,1,0:T(8,128)S(1)} %copy-done.3, bf16[1,5,96,1536]{3,2,1,0:T(8,128)(2,1)S(1)} %copy-done, bf16[1,5,96,1536]{3,2,1,0:T(8,128)(2,1)S(1)} %copy-done.1, bf16[1,96,1536]{2,1,0:T(8,128)(2,1)S(1)} %copy-done.2), custom_call_target="tpu_custom_call" | custom-call | flops 1660000000 | bytes 3700000 | tf_op jit(solution)/shard_map/hull_solve/pallas_call | solution.py:169
  147.3 0.7 copy.6
Async XLA Ops:
  0.0 1.4 copy-start
  1.4 1.4 copy-start.1
  2.7 1.0 copy-start.2
  3.7 0.9 copy-start.3

commit v2 on v1

--- a/solution.py
+++ b/solution.py
@@ -12,7 +12,14 @@
 ROWS = 96
 WIDTH = 128
 CHUNKS = 4
-FUSED = (0, 1, 2)
+FUSED = (0, 1)
+DIRECT = (4, 5)
+SPLIT = True
+ORDER = (
+    1, 2, 0, 3, 1, 0, 3, 0, 1, 2, 0, 3, 2, 1, 0, 2, 1, 0, 3, 1, 2, 0, 3, 1, 0, 2, 1, 3, 0, 2, 1, 3,
+    0, 2, 1, 3, 0, 2, 1, 3, 2, 0, 3, 2, 1, 0, 3, 1, 0, 1, 3, 2, 0, 3, 1, 2, 3, 2, 0, 3, 1, 2, 0, 1,
+    3, 0, 2, 1, 3, 2, 1, 3, 0, 2, 3, 1, 2, 0, 3, 2,
+)
 LAST = LEVELS
 
 
@@ -24,7 +31,7 @@
     return [(2 * LEVELS - 1, 0)]
 
 
-def kernel(load, lower, upper, inverse, out, fac, inv, cur, own, gat, fac_sem, z_sem, a_sem, b_sem, far_sem, send_sem, last_sem):
+def kernel(load, lower, upper, inverse, out, whole, fac, inv, cur, own, gat, fac_sem, z_sem, a_sem, b_sem, far_sem, send_sem, last_sem):
     frame = lax.axis_index("blk")
     row = lax.axis_index("row")
     x, y = row // SIDE, row % SIDE
@@ -32,6 +39,8 @@
     def device(shift, dx, dy):
         return ((frame + shift + FRAMES) % FRAMES, ((x + dx) % SIDE) * SIDE + (y + dy) % SIDE)
 
+    first = pltpu.make_async_copy(load.at[0], whole, fac_sem.at[3])
+    first.start()
     loads = [
         pltpu.make_async_copy(lower.at[0], fac.at[0], fac_sem.at[0]),
         pltpu.make_async_copy(upper.at[0], fac.at[1], fac_sem.at[1]),
@@ -87,8 +96,6 @@
                 send(own.at[level, c], gat.at[u, c, x, y], send_sem.at[level, c], z_sem.at[u, c], device(shift, 0, 0))
 
     def spread(level, c):
-        if level in FUSED or level == LAST:
-            return
         for i, (u, _) in enumerate(units(level)):
             turn = along(level, c, i)
             wait(gat.at[u, c, x, y], z_sem.at[u, c])
@@ -100,26 +107,37 @@
             turn = along(level, c, i)
             at = y if turn == 0 else x
             wait(line(u, c, turn, at, 0, SIDE if level in FUSED else SIDE - 1), a_sem.at[u, c])
-            for d in (1, SIDE - 1):
-                block = line(u, c, turn, at)
-                send(block, block, send_sem.at[level, c], b_sem.at[u, c], device(0, *step(1 - turn, d)))
+            if level in DIRECT:
+                for d in (2, 1, 3):
+                    block = line(u, c, turn, at)
+                    send(block, block, send_sem.at[level, c], far_sem.at[u, c], device(0, *step(1 - turn, d)))
+            elif SPLIT:
+                for sems, first in ((b_sem, 0), (far_sem, 2)):
+                    for d, half in ((1, first), (SIDE - 1, 2 - first)):
+                        block = line(u, c, turn, at, half, 2)
+                        send(block, block, send_sem.at[level, c], sems.at[u, c], device(0, *step(1 - turn, d)))
+            else:
+                for d in (1, SIDE - 1):
+                    block = line(u, c, turn, at)
+                    send(block, block, send_sem.at[level, c], b_sem.at[u, c], device(0, *step(1 - turn, d)))
 
     def relay(level, c):
         for i, (u, _) in enumerate(units(level)):
             turn = along(level, c, i)
             at = y if turn == 0 else x
-            wait(line(u, c, turn, pl.ds(0, 2)), b_sem.at[u, c])
-            for half, d in ((0, 1), (1, SIDE - 1)):
-                block = line(u, c, turn, (at + SIDE - d) % SIDE, half * 2, 2)
+            wait(line(u, c, turn, 0 if SPLIT else pl.ds(0, 2)), b_sem.at[u, c])
+            for half, d in ((0, 1), (2, SIDE - 1)):
+                block = line(u, c, turn, (at + SIDE - d) % SIDE, half, 2)
                 send(block, block, send_sem.at[level, c], far_sem.at[u, c], device(0, *step(1 - turn, d)))
 
     def product(block, u, c):
         return jnp.dot(block, gat[u, c].reshape(SIDE * SIDE * ROWS, WIDTH), preferred_element_type=jnp.float32)
 
-    def finish(level, c):
-        for i, (u, _) in enumerate(units(level)):
-            turn = along(level, c, i)
-            wait(line(u, c, turn, 0), far_sem.at[u, c])
+    def close(level, c):
+        for i, (u, _) in enumerate(units(level)):
+            turn = along(level, c, i)
+            blocks = 3 if level in DIRECT else 2 if SPLIT else 1
+            wait(line(u, c, turn, pl.ds(0, blocks)), far_sem.at[u, c])
         if level < LEVELS - 1:
             total = cur[c]
             (u, shift), (v, _) = units(level)
@@ -133,25 +151,28 @@
         else:
             u, _ = units(level)[0]
             out[0, :, pl.ds(c * WIDTH, WIDTH)] = product(inv[...], u, c)
-
+        if level < LAST:
+            begin(level + 1, c)
+
+    steps = [(begin, 0)]
+    for level in range(LEVELS + 1):
+        if level not in FUSED and level != LAST:
+            steps.append((spread, level))
+        steps.append((cross, level))
+        if level not in DIRECT:
+            steps.append((relay, level))
+        steps.append((close, level))
+
+    first.wait()
     for c in range(CHUNKS):
-        cur[c] = load[0, :, pl.ds(c * WIDTH, WIDTH)]
-    pl.semaphore_wait(barrier, len(partners))
-    for c in range(CHUNKS):
-        begin(0, c)
+        cur[c] = whole[:, pl.ds(c * WIDTH, WIDTH)]
     for copy in loads:
         copy.wait()
-    for level in range(LEVELS + 1):
-        for c in range(CHUNKS):
-            spread(level, c)
-        for c in range(CHUNKS):
-            cross(level, c)
-        for c in range(CHUNKS):
-            relay(level, c)
-        for c in range(CHUNKS):
-            finish(level, c)
-            if level < LAST:
-                begin(level + 1, c)
+    pl.semaphore_wait(barrier, len(partners))
+    todo = [iter(steps) for _ in range(CHUNKS)]
+    for c in ORDER:
+        act, level = next(todo[c])
+        act(level, c)
     for level in range(LEVELS + 1):
         for c in range(CHUNKS):
             u = units(level)[0][0]
@@ -169,15 +190,16 @@
     return pl.pallas_call(
         kernel,
         out_shape=jax.ShapeDtypeStruct((1, ROWS, CHUNKS * WIDTH), jnp.float32),
-        in_specs=[pl.BlockSpec(memory_space=pltpu.VMEM)] + [pl.BlockSpec(memory_space=pl.ANY)] * 3,
+        in_specs=[pl.BlockSpec(memory_space=pl.ANY)] * 4,
         out_specs=pl.BlockSpec(memory_space=pltpu.VMEM),
         scratch_shapes=[
+            pltpu.VMEM((ROWS, CHUNKS * WIDTH), jnp.float32),
             pltpu.VMEM((2, LEVELS, ROWS, SIDE * SIDE * ROWS), jnp.bfloat16),
             pltpu.VMEM((ROWS, SIDE * SIDE * ROWS), jnp.bfloat16),
             pltpu.VMEM((CHUNKS, ROWS, WIDTH), jnp.float32),
             pltpu.VMEM((LEVELS, CHUNKS, ROWS, WIDTH), jnp.bfloat16),
             pltpu.VMEM((count, CHUNKS, SIDE, SIDE, ROWS, WIDTH), jnp.bfloat16),
-            pltpu.SemaphoreType.DMA((3,)),
+            pltpu.SemaphoreType.DMA((4,)),
             pltpu.SemaphoreType.DMA((count, CHUNKS)),
             pltpu.SemaphoreType.DMA((count, CHUNKS)),
             pltpu.SemaphoreType.DMA((count, CHUNKS)),
@@ -185,7 +207,7 @@
             pltpu.SemaphoreType.DMA((LEVELS + 1, CHUNKS)),
             pltpu.SemaphoreType.DMA((CHUNKS,)),
         ],
-        compiler_params=pltpu.CompilerParams(collective_id=0, has_side_effects=True, vmem_limit_bytes=48 * 2**20),
+        compiler_params=pltpu.CompilerParams(collective_id=0, has_side_effects=True, vmem_limit_bytes=62 * 2**20),
         cost_estimate=pl.CostEstimate(flops=1_660_000_000, bytes_accessed=3_700_000, transcendentals=0),
         name="hull_solve",
     )(load_cases, lower_factor, upper_factor, inverse)

time: 148 us -> 129 us (0.87)
  Pallas kernels: 143 us -> 127 us
  local copies, waits for them, and re-layouts: 5.31 us -> 1.62 us
    pallas_call x1, Pallas kernels: 143 us -> 127 us  [per_device(): pl.pallas_call(kernel, out_shape=jax.ShapeDtypeStruct((1, ROWS, CHUNKS *...]
    unnamed x9 -> x1, local copies, waits for them, and re-layouts: 5.31 us -> 1.62 us
where the time goes in v2:
time: 129 us
  Pallas kernels  127 us (98%)
  local copies, waits for them, and re-layouts  1.62 us (1%)
    pallas_call x1, Pallas kernels, per_device(): pl.pallas_call(kernel, out_shape=jax.ShapeDtypeStruct((1, ROWS, CHUNKS *...  127 us

profile of v2, /device:TPU:2, one launch (start us, length us, event | category | flops | bytes accessed | tf_op | source)
XLA Modules:
  0.0 128.9 jit_solution(16691158108976396537)
XLA Ops:
  0.0 127.3 %hull_solve.1 = f32[1,96,512]{2,1,0:T(8,128)} custom-call(f32[1,96,512]{2,1,0:T(8,128)} %load.1, bf16[1,5,96,1536]{3,2,1,0:T(8,128)(2,1)} %lower.1, bf16[1,5,96,1536]{3,2,1,0:T(8,128)(2,1)} %upper.1, bf16[1,96,1536]{2,1,0:T(8,128)(2,1)} %inverse.1), custom_call_target="tpu_custom_call" | custom-call | flops 1660000000 | bytes 3700000 | tf_op jit(solution)/shard_map/hull_solve/pallas_call | solution.py:190
  127.3 1.6 %copy.6 = f32[1,96,512]{2,1,0:T(8,128)} copy(f32[1,96,512]{2,1,0:T(8,128)} %hull_solve.1) | data formatting | bytes 393216

commit v3 on v2

--- a/solution.py
+++ b/solution.py
@@ -50,7 +50,7 @@
         copy.start()
 
     partners = {(0, d, 0) for d in range(1, SIDE)} | {(0, 0, d) for d in range(1, SIDE)}
-    for level in range(LEVELS):
+    for level in range(2):
         for _, shift in units(level):
             partners.add((shift, 0, 0))
             if level in FUSED:
@@ -133,7 +133,13 @@
     def product(block, u, c):
         return jnp.dot(block, gat[u, c].reshape(SIDE * SIDE * ROWS, WIDTH), preferred_element_type=jnp.float32)
 
+    waited = []
+
     def close(level, c):
+        if not waited:
+            waited.append(1)
+            for copy in loads:
+                copy.wait()
         for i, (u, _) in enumerate(units(level)):
             turn = along(level, c, i)
             blocks = 3 if level in DIRECT else 2 if SPLIT else 1
@@ -166,8 +172,6 @@
     first.wait()
     for c in range(CHUNKS):
         cur[c] = whole[:, pl.ds(c * WIDTH, WIDTH)]
-    for copy in loads:
-        copy.wait()
     pl.semaphore_wait(barrier, len(partners))
     todo = [iter(steps) for _ in range(CHUNKS)]
     for c in ORDER:

time: 129 us -> 127 us (0.984)
  the two profiles are of different devices: /device:TPU:2 before, /device:TPU:32 now
where the time goes in v3:
time: 127 us; the launch traced here: 126 us
  Pallas kernels  125 us (98%)
  local copies, waits for them, and re-layouts  1.62 us (1%)
    pallas_call x1, Pallas kernels, per_device(): pl.pallas_call(kernel, out_shape=jax.ShapeDtypeStruct((1, ROWS, CHUNKS *...  125 us

profile of v3, /device:TPU:32, one launch (start us, length us, event | category | flops | bytes accessed | tf_op | source)
XLA Modules:
  0.0 126.4 jit_solution(11361764211414789669)
XLA Ops:
  0.0 124.8 %hull_solve.1 = f32[1,96,512]{2,1,0:T(8,128)} custom-call(f32[1,96,512]{2,1,0:T(8,128)} %load.1, bf16[1,5,96,1536]{3,2,1,0:T(8,128)(2,1)} %lower.1, bf16[1,5,96,1536]{3,2,1,0:T(8,128)(2,1)} %upper.1, bf16[1,96,1536]{2,1,0:T(8,128)(2,1)} %inverse.1), custom_call_target="tpu_custom_call" | custom-call | flops 1660000000 | bytes 3700000 | tf_op jit(solution)/shard_map/hull_solve/pallas_call | solution.py:194
  124.8 1.6 %copy.6 = f32[1,96,512]{2,1,0:T(8,128)} copy(f32[1,96,512]{2,1,0:T(8,128)} %hull_solve.1) | data formatting | bytes 393216

commit v4 on v3

--- a/solution.py
+++ b/solution.py
@@ -16,9 +16,9 @@
 DIRECT = (4, 5)
 SPLIT = True
 ORDER = (
-    1, 2, 0, 3, 1, 0, 3, 0, 1, 2, 0, 3, 2, 1, 0, 2, 1, 0, 3, 1, 2, 0, 3, 1, 0, 2, 1, 3, 0, 2, 1, 3,
-    0, 2, 1, 3, 0, 2, 1, 3, 2, 0, 3, 2, 1, 0, 3, 1, 0, 1, 3, 2, 0, 3, 1, 2, 3, 2, 0, 3, 1, 2, 0, 1,
-    3, 0, 2, 1, 3, 2, 1, 3, 0, 2, 3, 1, 2, 0, 3, 2,
+    0, 1, 2, 3, 0, 1, 0, 2, 1, 0, 2, 3, 1, 0, 3, 2, 0, 1, 3, 2, 0, 1, 0, 2, 3, 1, 0, 2, 1, 3, 0, 2,
+    1, 3, 0, 2, 1, 3, 2, 0, 1, 3, 2, 0, 3, 1, 0, 3, 2, 1, 0, 2, 3, 1, 2, 3, 0, 1, 2, 3, 0, 3, 1, 2,
+    1, 3, 2, 0, 3, 1, 0, 2, 1, 3, 2, 0, 3, 2, 1, 3,
 )
 LAST = LEVELS
 

time: 127 us -> 123 us (0.969)
  Pallas kernels: 125 us -> 122 us
    pallas_call x1, Pallas kernels: 125 us -> 122 us  [per_device(): pl.pallas_call(kernel, out_shape=jax.ShapeDtypeStruct((1, ROWS, CHUNKS *...]
where the time goes in v4:
time: 123 us
  Pallas kernels  122 us (99%)
  local copies, waits for them, and re-layouts  1.62 us (1%)
    pallas_call x1, Pallas kernels, per_device(): pl.pallas_call(kernel, out_shape=jax.ShapeDtypeStruct((1, ROWS, CHUNKS *...  122 us

profile of v4, /device:TPU:32, one launch (start us, length us, event | category | flops | bytes accessed | tf_op | source)
XLA Modules:
  0.0 123.2 jit_solution(6823452507322815632)
XLA Ops:
  0.0 121.6 %hull_solve.1 = f32[1,96,512]{2,1,0:T(8,128)} custom-call(f32[1,96,512]{2,1,0:T(8,128)} %load.1, bf16[1,5,96,1536]{3,2,1,0:T(8,128)(2,1)} %lower.1, bf16[1,5,96,1536]{3,2,1,0:T(8,128)(2,1)} %upper.1, bf16[1,96,1536]{2,1,0:T(8,128)(2,1)} %inverse.1), custom_call_target="tpu_custom_call" | custom-call | flops 1660000000 | bytes 3700000 | tf_op jit(solution)/shard_map/hull_solve/pallas_call | solution.py:194
  121.6 1.6 %copy.6 = f32[1,96,512]{2,1,0:T(8,128)} copy(f32[1,96,512]{2,1,0:T(8,128)} %hull_solve.1) | data formatting | bytes 393216

commit v5 on v4

--- a/solution.py
+++ b/solution.py
@@ -16,9 +16,9 @@
 DIRECT = (4, 5)
 SPLIT = True
 ORDER = (
-    0, 1, 2, 3, 0, 1, 0, 2, 1, 0, 2, 3, 1, 0, 3, 2, 0, 1, 3, 2, 0, 1, 0, 2, 3, 1, 0, 2, 1, 3, 0, 2,
-    1, 3, 0, 2, 1, 3, 2, 0, 1, 3, 2, 0, 3, 1, 0, 3, 2, 1, 0, 2, 3, 1, 2, 3, 0, 1, 2, 3, 0, 3, 1, 2,
-    1, 3, 2, 0, 3, 1, 0, 2, 1, 3, 2, 0, 3, 2, 1, 3,
+    0, 1, 2, 3, 0, 1, 0, 2, 1, 0, 3, 2, 1, 0, 3, 2, 1, 0, 3, 1, 2, 0, 3, 1, 2, 0, 3, 1, 0, 3, 1, 2,
+    0, 3, 1, 2, 0, 3, 1, 2, 3, 0, 2, 1, 3, 0, 2, 1, 0, 3, 1, 2, 0, 3, 1, 2, 3, 2, 0, 3, 1, 2, 0, 1,
+    3, 0, 2, 3, 1, 2, 1, 3, 0, 2, 3, 2, 1, 3, 0, 2,
 )
 LAST = LEVELS
 

time: 123 us -> 123 us (level)
  no operation moved by 1% of the time
where the time goes in v5:
time: 123 us
  Pallas kernels  121 us (98%)
  local copies, waits for them, and re-layouts  1.62 us (1%)
    pallas_call x1, Pallas kernels, per_device(): pl.pallas_call(kernel, out_shape=jax.ShapeDtypeStruct((1, ROWS, CHUNKS *...  121 us

profile of v5, /device:TPU:32, one launch (start us, length us, event | category | flops | bytes accessed | tf_op | source)
XLA Modules:
  0.0 122.6 jit_solution(15636238329848143675)
XLA Ops:
  0.0 120.9 %hull_solve.1 = f32[1,96,512]{2,1,0:T(8,128)} custom-call(f32[1,96,512]{2,1,0:T(8,128)} %load.1, bf16[1,5,96,1536]{3,2,1,0:T(8,128)(2,1)} %lower.1, bf16[1,5,96,1536]{3,2,1,0:T(8,128)(2,1)} %upper.1, bf16[1,96,1536]{2,1,0:T(8,128)(2,1)} %inverse.1), custom_call_target="tpu_custom_call" | custom-call | flops 1660000000 | bytes 3700000 | tf_op jit(solution)/shard_map/hull_solve/pallas_call | solution.py:194
  121.0 1.6 %copy.6 = f32[1,96,512]{2,1,0:T(8,128)} copy(f32[1,96,512]{2,1,0:T(8,128)} %hull_solve.1) | data formatting | bytes 393216

commit v6 on v5

--- a/solution.py
+++ b/solution.py
@@ -16,9 +16,9 @@
 DIRECT = (4, 5)
 SPLIT = True
 ORDER = (
-    0, 1, 2, 3, 0, 1, 0, 2, 1, 0, 3, 2, 1, 0, 3, 2, 1, 0, 3, 1, 2, 0, 3, 1, 2, 0, 3, 1, 0, 3, 1, 2,
-    0, 3, 1, 2, 0, 3, 1, 2, 3, 0, 2, 1, 3, 0, 2, 1, 0, 3, 1, 2, 0, 3, 1, 2, 3, 2, 0, 3, 1, 2, 0, 1,
-    3, 0, 2, 3, 1, 2, 1, 3, 0, 2, 3, 2, 1, 3, 0, 2,
+    1, 3, 0, 2, 1, 0, 1, 2, 0, 1, 3, 2, 0, 3, 1, 2, 0, 1, 3, 0, 2, 1, 3, 0, 2, 1, 3, 0, 2, 1, 3, 0,
+    1, 2, 0, 3, 1, 2, 0, 3, 2, 1, 3, 0, 2, 1, 3, 0, 1, 2, 0, 3, 1, 2, 0, 3, 2, 3, 1, 2, 0, 3, 1, 0,
+    2, 1, 3, 2, 0, 3, 0, 2, 1, 3, 2, 0, 3, 1, 2, 3,
 )
 LAST = LEVELS
 
@@ -86,7 +86,8 @@
             for d in (2, 1, 3):
                 send(gat.at[u, c, x, y], gat.at[u, c, x, y], last_sem.at[c], a_sem.at[u, c], device(0, *step(turn, d)))
             return
-        own[level, c] = value
+        if level > 0:
+            own[level, c] = value
         for i, (u, shift) in enumerate(units(level)):
             turn = along(level, c, i)
             if level in FUSED:
@@ -172,6 +173,7 @@
     first.wait()
     for c in range(CHUNKS):
         cur[c] = whole[:, pl.ds(c * WIDTH, WIDTH)]
+        own[0, c] = cur[c].astype(jnp.bfloat16)
     pl.semaphore_wait(barrier, len(partners))
     todo = [iter(steps) for _ in range(CHUNKS)]
     for c in ORDER:

time: 123 us -> 123 us (level)
  no operation moved by 1% of the time
where the time goes in v6:
time: 123 us; the launch traced here: 122 us
  Pallas kernels  121 us (98%)
  local copies, waits for them, and re-layouts  1.62 us (1%)
    pallas_call x1, Pallas kernels, per_device(): pl.pallas_call(kernel, out_shape=jax.ShapeDtypeStruct((1, ROWS, CHUNKS *...  121 us

profile of v6, /device:TPU:32, one launch (start us, length us, event | category | flops | bytes accessed | tf_op | source)
XLA Modules:
  0.0 122.4 jit_solution(1959237207215782695)
XLA Ops:
  0.0 120.8 %hull_solve.1 = f32[1,96,512]{2,1,0:T(8,128)} custom-call(f32[1,96,512]{2,1,0:T(8,128)} %load.1, bf16[1,5,96,1536]{3,2,1,0:T(8,128)(2,1)} %lower.1, bf16[1,5,96,1536]{3,2,1,0:T(8,128)(2,1)} %upper.1, bf16[1,96,1536]{2,1,0:T(8,128)(2,1)} %inverse.1), custom_call_target="tpu_custom_call" | custom-call | flops 1660000000 | bytes 3700000 | tf_op jit(solution)/shard_map/hull_solve/pallas_call | solution.py:196
  120.8 1.6 %copy.6 = f32[1,96,512]{2,1,0:T(8,128)} copy(f32[1,96,512]{2,1,0:T(8,128)} %hull_solve.1) | data formatting | bytes 393216
